TPU v7x, 512 devices: a whole 4x8x8 slice. The times are simulated.
512 devices in a mesh: stream: 32 (over z_hi, y, core), azi: 16 (over z_lo, x).
Axes of the slice: x: 4, y: 8, z: 8 (z_hi: 2, z_lo: 4; z = z_hi * 4 + z_lo), core: 2. Of those that a mesh axis runs over, the one named last changes fastest.
Arguments:
- velocity: float32 [3, 64, 256, 2048], P(None, 'stream', None, 'azi'), may hold values from -6 to 6
- mean_flow: float32 [256], replicated, may hold values from 0.5 to 1.5
- part_x: int32 [32, 16, 16, 128], P('stream', 'azi'), may hold values from 0 to 1
- part_r: int32 [32, 16, 16, 128], P('stream', 'azi'), may hold values from 0 to 255
- part_t: int32 [32, 16, 16, 128], P('stream', 'azi'), may hold values from 0 to 127
- part_vel: float32 [32, 16, 16, 3, 128], P('stream', 'azi'), may hold values from -6 to 6
- part_rate: float32 [32, 16, 16, 128], P('stream', 'azi'), may hold values from 0.5 to 5
- counts: int32 [32, 16, 16], P('stream', 'azi'), may hold values from 1 to 128, as said below
Outputs:
- new_velocity: float32 [3, 64, 256, 2048], P(None, 'stream', None, 'azi')
- new_part_vel: float32 [32, 16, 16, 3, 128], P('stream', 'azi')
Inputs may be any that keep to these rules, and one draw needn't show every extreme that they name: `counts`: in every source slab and source device, at least one block is full (128 live); in each streamwise group some owner receives a full block from every source device.
All inputs are finite; a program needn't handle non-finite values.
Results may differ from a plain program's by a relative error of at most 0.00002.
Values sent between devices are 32-bit elements; how exact they have to be, the bound alone decides.
A program may use at most 128 MiB of HBM per device.

v0:
```python
import jax
import jax.numpy as jnp
from jax import lax
from jax.sharding import PartitionSpec as P


def with_halo(cells, sides, width):
    for axis, dim in sides:
        count = lax.axis_size(axis)
        head = lax.slice_in_dim(cells, 0, width, axis=dim)
        tail = lax.slice_in_dim(cells, cells.shape[dim] - width, cells.shape[dim], axis=dim)
        cells = jnp.concatenate(
            [
                lax.ppermute(tail, axis, [(i, (i + 1) % count) for i in range(count)]),
                cells,
                lax.ppermute(head, axis, [((i + 1) % count, i) for i in range(count)]),
            ],
            axis=dim,
        )
    return cells


def body(velocity, mean_flow, part_x, part_r, part_t, part_vel, part_rate, counts):
    planes, count_r, cells_t = (velocity.shape[1], velocity.shape[2], velocity.shape[3])
    owners, slots = (part_rate.shape[2], part_rate.shape[3])
    slot_ids = jnp.arange(slots, dtype=jnp.int32)
    live = (slot_ids[None, None, None, :] < counts[..., None]).astype(jnp.float32)
    rate = part_rate * live
    cell_ids = (part_x * count_r + part_r) * cells_t + part_t
    records = jnp.concatenate([part_vel, rate[:, :, :, None, :]], axis=3)
    every_rec, every_cell = (
        lax.all_gather(records, "azi", axis=1, tiled=True),
        lax.all_gather(cell_ids, "azi", axis=1, tiled=True),
    )
    mine = lax.axis_index("azi")
    got_rec = lax.dynamic_index_in_dim(every_rec, mine, 2, keepdims=False)[None]
    got_cell = lax.dynamic_index_in_dim(every_cell, mine, 2, keepdims=False)[None]
    incoming_vel = got_rec[0, 0, :, :3, :]
    incoming_rate = got_rec[0, 0, :, 3, :]
    flat_index = got_cell[0, 0].reshape(-1)
    flat_field = velocity.reshape(3, -1)
    fluid_at = jnp.transpose(flat_field[:, flat_index].reshape(3, owners, slots), (1, 0, 2))
    kick = 0.1 * incoming_rate[:, None, :] * (fluid_at - incoming_vel)
    updated = (incoming_vel + kick)[None, None]
    new_part_vel = lax.all_to_all(updated, "azi", split_axis=2, concat_axis=2, tiled=True)
    pushes = (-0.5 * jnp.transpose(kick, (1, 0, 2))).reshape(3, -1)
    deposit = jnp.zeros_like(flat_field).at[:, flat_index].add(pushes).reshape(velocity.shape)
    padded = with_halo(velocity, (("stream", 1), ("azi", 3)), 1)
    x_plus = padded[:, 2:, :, 1:-1]
    x_minus = padded[:, :-2, :, 1:-1]
    t_plus = padded[:, 1:-1, :, 2:]
    t_minus = padded[:, 1:-1, :, :-2]
    radial_pad = jnp.pad(velocity, ((0, 0), (0, 0), (1, 1), (0, 0)))
    r_plus = radial_pad[:, :, 2:, :]
    r_minus = radial_pad[:, :, :-2, :]
    j_index = jnp.arange(count_r, dtype=jnp.float32)
    radius = 0.5 + 0.5 * (j_index + 0.5) / count_r
    h_term = (0.25 / (count_r * radius))[None, None, :, None]
    k_term = ((0.75 / radius) ** 2)[None, None, :, None]
    lap = (
        x_plus
        + x_minus
        - 2.0 * velocity
        + (1.0 + h_term) * r_plus
        + (1.0 - h_term) * r_minus
        - 2.0 * velocity
    )
    lap = lap + k_term * (t_plus + t_minus - 2.0 * velocity)
    advect = -0.15 * mean_flow[None, None, :, None] * (x_plus - x_minus)
    new_velocity = velocity + 0.08 * lap + advect + deposit
    return (new_velocity, new_part_vel)


def solution(mesh):
    in_specs = (
        P(None, "stream", None, "azi"),
        P(),
        P("stream", "azi", None, None),
        P("stream", "azi", None, None),
        P("stream", "azi", None, None),
        P("stream", "azi", None, None, None),
        P("stream", "azi", None, None),
        P("stream", "azi", None),
    )
    out_specs = (P(None, "stream", None, "azi"), P("stream", "azi", None, None, None))
    return jax.shard_map(body, mesh=mesh, in_specs=in_specs, out_specs=out_specs, check_vma=False)
```

profile of v0, /device:TPU:6, one launch (start us, length us, event | category | flops | bytes accessed | tf_op | source)
XLA Modules:
  0.0 210.1 jit_solution(12891404227901747454)
XLA Ops:
  0.6 1.2 fusion.15
  1.9 1.9 collective-permute-start.1
  3.8 13.3 %collective-permute-start = (f32[3,1,256,128]{3,2,1,0:T(8,128)S(1)}, f32[3,1,256,128]{3,2,1,0:T(8,128)S(1)}, u32[]{:S(2)}, u32[]{:S(2)}) collective-permute-start(f32[3,1,256,128]{3,2,1,0:T(8,128)S(1)} %get-tuple-element.12), channel_id=1, source_target_pairs={{16,0},{32,16},{48,32},{64,48},{80,64},{96,80},{112,96},{128,112},... | collective-permute-start | bytes 1179656 | tf_op jit(solution)/shard_map/ppermute | solution.py:16
  17.1 0.0 copy-start.4
  17.1 0.0 copy-start.5
  17.1 0.0 copy-start.6
  17.1 16.4 %copy.76 = f32[3,2,256,128]{0,3,2,1:T(8,128)} copy(f32[3,2,256,128]{3,2,1,0:T(8,128)S(1)} %copy-done) | data formatting | bytes 1572864 | tf_op args[0]
  33.6 35.1 %all_gather.6 = s32[1,16,16,128]{3,2,0,1:T(8,128)S(1)} all-gather(s32[1,1,16,128]{3,2,0,1:T(8,128)S(1)} %bitcast_add_fusion), channel_id=1, replica_groups=mesh['stream'=32,'azi'=16] {'azi'}, dimensions={1}, use_global_device_ids=true | all-gather | bytes 139264 | tf_op jit(solution)/shard_map/all_gather | solution.py:33
  68.7 16.0 %gather_fusion = f32[2048,3]{1,0:T(8,128)S(1)} fusion(f32[3,65536]{0,1:T(8,128)} %bitcast.53, s32[2048]{0:T(1024)S(1)} %broadcast_clamp_fusion), kind=kCustom, calls=%fused_computation | custom fusion | bytes 57344 | tf_op jit(solution)/shard_map/gather | solution.py:42
  84.7 0.3 copy.77
  85.1 0.7 select_bitcast_fusion
  85.8 0.7 pad_maximum_fusion.4
  86.6 43.3 %all_gather.7 = f32[1,16,16,4,128]{4,2,3,0,1:T(8,128)S(1)} all-gather(f32[1,1,16,4,128]{4,2,3,0,1:T(8,128)S(1)} %pad_maximum_fusion.4), channel_id=1, replica_groups=mesh['stream'=32,'azi'=16] {'azi'}, dimensions={1}, use_global_device_ids=true | all-gather | bytes 557056 | tf_op jit(solution)/shard_map/all_gather | solution.py:32
  129.9 0.6 add_bitcast_fusion
  130.5 8.7 %all-to-all-start = ((f32[1,1,16,3,128]{4,3,1,0,2:T(4,128)}), f32[1,1,16,3,128]{4,3,1,0,2:T(4,128)}, u32[]{:S(2)}, u32[]{:S(2)}) async-start(f32[1,1,16,3,128]{4,3,1,0,2:T(4,128)} %get-tuple-element.14), calls=%async_computation | async-start | bytes 65536 | tf_op jit(solution)/shard_map/all_to_all | solution.py:45
  139.2 0.7 divide_multiply_fusion
  139.9 0.1 constant_dynamic-update-slice_fusion.1
  140.1 2.2 %fusion.14 = (f32[3,4,256,1]{3,2,1,0:T(8,128)}, f32[3,4,256,1]{3,2,1,0:T(8,128)}) fusion(f32[3,4,256,128]{3,2,1,0:T(8,128)S(1)} %constant_dynamic-update-slice_fusion), kind=kLoop, calls=%fused_computation.44 | loop fusion | bytes 49152 | tf_op jit(solution)/shard_map/slice | solution.py:10
  142.3 2.5 %copy.68 = f32[3,4,256,1]{2,1,3,0:T(4,128)} copy(f32[3,4,256,1]{3,2,1,0:T(8,128)} %get-tuple-element.10) | data formatting | bytes 24576 | tf_op jit(solution)/shard_map/slice | solution.py:10
  144.7 2.7 %collective-permute-start.2 = (f32[3,4,256,1]{2,1,3,0:T(4,128)}, f32[3,4,256,1]{2,1,3,0:T(4,128)}, u32[]{:S(2)}, u32[]{:S(2)}) collective-permute-start(f32[3,4,256,1]{2,1,3,0:T(4,128)} %copy.68), channel_id=1, source_target_pairs={{1,0},{2,1},{3,2},{4,3},{5,4},{6,5},{7,6},{8,7},{9,8},{10,9},{11,1... | collective-permute-start | bytes 36872 | tf_op jit(solution)/shard_map/ppermute | solution.py:16
  147.5 2.5 %copy.70 = f32[3,4,256,1]{2,1,3,0:T(4,128)} copy(f32[3,4,256,1]{3,2,1,0:T(8,128)} %get-tuple-element.11) | data formatting | bytes 24576 | tf_op jit(solution)/shard_map/slice | solution.py:11
  150.0 5.2 %collective-permute-start.3 = (f32[3,4,256,1]{2,1,3,0:T(4,128)}, f32[3,4,256,1]{2,1,3,0:T(4,128)}, u32[]{:S(2)}, u32[]{:S(2)}) collective-permute-start(f32[3,4,256,1]{2,1,3,0:T(4,128)} %copy.70), channel_id=1, source_target_pairs={{0,1},{1,2},{2,3},{3,4},{4,5},{5,6},{6,7},{7,8},{8,9},{9,10},{10,1... | collective-permute-start | bytes 36872 | tf_op jit(solution)/shard_map/ppermute | solution.py:14
  155.2 0.6 broadcast_subtract_fusion
  155.8 1.4 copy.78
  157.1 25.0 %scatter_custom_fusion = f32[3,65536]{0,1:T(8,128)} fusion(s32[2048]{0:T(1024)S(1)} %bitcast.59, f32[2048,3]{1,0:T(8,128)} %copy.78, f32[]{:T(128)} %constant.13.clone.1), kind=kCustom, calls=%fused_computation.2 | custom fusion | flops 6144 | bytes 786944 | tf_op jit(solution)/shard_map/scatter-add | solution.py:47
  182.1 18.6 %copy.81 = f32[3,2,256,128]{3,2,1,0:T(8,128)S(1)} copy(f32[3,2,256,128]{0,3,2,1:T(8,128)} %bitcast.52) | data formatting | bytes 1572864 | tf_op jit(solution)/shard_map/reshape | solution.py:47
  200.8 1.4 copy.80
  202.1 0.0 collective-permute-done.2
  202.1 2.4 %copy.69 = f32[3,4,256,1]{3,2,1,0:T(8,128)} copy(f32[3,4,256,1]{2,1,3,0:T(4,128)} %collective-permute-done.2) | data formatting | bytes 24576 | tf_op jit(solution)/shard_map/ppermute | solution.py:16
  204.5 0.0 collective-permute-done.3
  204.5 2.4 %copy.71 = f32[3,4,256,1]{3,2,1,0:T(8,128)} copy(f32[3,4,256,1]{2,1,3,0:T(4,128)} %collective-permute-done.3) | data formatting | bytes 24576 | tf_op jit(solution)/shard_map/ppermute | solution.py:14
  206.9 3.2 %fusion.9 = f32[3,2,256,128]{3,2,1,0:T(8,128)} fusion(f32[3,2,256,128]{3,2,1,0:T(8,128)S(1)} %copy.81, f32[3,2,256,128]{3,2,1,0:T(8,128)S(1)} %copy-done, f32[3,4,256,128]{3,2,1,0:T(8,128)S(1)} %constant_dynamic-update-slice_fusion, f32[3,4,256,1]{3,2,1,0:T(8,128)} %copy.71, f32[3,4,256,1]{3,2,1,0:T(8,128)} %copy.69, f32[3,1,256,128]{3,2,1,0:T(8,128)} %copy-done.1, ...), kind=kLoop, calls=%fused_computation.12 | loop fusion | flops 4325376 | bytes 4747264 | tf_op jit(solution)/shard_map/add | solution.py:70
  (25 shorter events, 0.2 us)
Async XLA Ops:
  0.6 16.5 %copy-start = (f32[3,2,256,128]{3,2,1,0:T(8,128)S(1)}, f32[3,2,256,128]{3,2,1,0:T(8,128)}, u32[]{:S(2)}) copy-start(f32[3,2,256,128]{3,2,1,0:T(8,128)} %param.8) | copy-start | bytes 2359300
  1.9 138.0 %collective-permute-start.1 = (f32[3,1,256,128]{3,2,1,0:T(8,128)S(1)}, f32[3,1,256,128]{3,2,1,0:T(8,128)S(1)}, u32[]{:S(2)}, u32[]{:S(2)}) collective-permute-start(f32[3,1,256,128]{3,2,1,0:T(8,128)S(1)} %get-tuple-element.13), channel_id=1, source_target_pairs={{0,16},{16,32},{32,48},{48,64},{64,80},{80,96},{96,112},{112,128},... | collective-permute-start | bytes 1179656 | tf_op jit(solution)/shard_map/ppermute | solution.py:14
  3.8 136.2 %collective-permute-start = (f32[3,1,256,128]{3,2,1,0:T(8,128)S(1)}, f32[3,1,256,128]{3,2,1,0:T(8,128)S(1)}, u32[]{:S(2)}, u32[]{:S(2)}) collective-permute-start(f32[3,1,256,128]{3,2,1,0:T(8,128)S(1)} %get-tuple-element.12), channel_id=1, source_target_pairs={{16,0},{32,16},{48,32},{64,48},{80,64},{96,80},{112,96},{128,112},... | collective-permute-start | bytes 1179656 | tf_op jit(solution)/shard_map/ppermute | solution.py:16
  17.1 16.5 %copy-start.4 = (s32[1,1,16,128]{3,2,1,0:T(8,128)S(1)}, s32[1,1,16,128]{3,2,1,0:T(8,128)}, u32[]{:S(2)}) copy-start(s32[1,1,16,128]{3,2,1,0:T(8,128)} %param.12) | copy-start | bytes 24580
  17.1 16.5 %copy-start.5 = (s32[1,1,16,128]{3,2,1,0:T(8,128)S(1)}, s32[1,1,16,128]{3,2,1,0:T(8,128)}, u32[]{:S(2)}) copy-start(s32[1,1,16,128]{3,2,1,0:T(8,128)} %param.11) | copy-start | bytes 24580
  17.1 16.4 %copy-start.6 = (s32[1,1,16,128]{3,2,1,0:T(8,128)S(1)}, s32[1,1,16,128]{3,2,1,0:T(8,128)}, u32[]{:S(2)}) copy-start(s32[1,1,16,128]{3,2,1,0:T(8,128)} %param.10) | copy-start | bytes 24580
  33.6 51.5 %copy-start.3 = (f32[1,1,16,128]{3,2,1,0:T(8,128)S(1)}, f32[1,1,16,128]{3,2,1,0:T(8,128)}, u32[]{:S(2)}) copy-start(f32[1,1,16,128]{3,2,1,0:T(8,128)} %param.14) | copy-start | bytes 24580
  130.5 70.2 %all-to-all-start = ((f32[1,1,16,3,128]{4,3,1,0,2:T(4,128)}), f32[1,1,16,3,128]{4,3,1,0,2:T(4,128)}, u32[]{:S(2)}, u32[]{:S(2)}) async-start(f32[1,1,16,3,128]{4,3,1,0,2:T(4,128)} %get-tuple-element.14), calls=%async_computation | async-start | bytes 65536 | tf_op jit(solution)/shard_map/all_to_all | solution.py:45
  140.0 2.2 %copy-start.1 = (f32[3,1,256,128]{3,2,1,0:T(8,128)}, f32[3,1,256,128]{3,2,1,0:T(8,128)S(1)}, u32[]{:S(2)}) copy-start(f32[3,1,256,128]{3,2,1,0:T(8,128)S(1)} %collective-permute-done) | copy-start | bytes 1179652
  142.3 13.5 %copy-start.2 = (f32[2048,3]{0,1:T(4,128)S(1)}, f32[2048,3]{0,1:T(4,128)}, u32[]{:S(2)}) copy-start(f32[2048,3]{0,1:T(4,128)} %get-tuple-element.15) | copy-start | bytes 73732
  144.7 57.4 %collective-permute-start.2 = (f32[3,4,256,1]{2,1,3,0:T(4,128)}, f32[3,4,256,1]{2,1,3,0:T(4,128)}, u32[]{:S(2)}, u32[]{:S(2)}) collective-permute-start(f32[3,4,256,1]{2,1,3,0:T(4,128)} %copy.68), channel_id=1, source_target_pairs={{1,0},{2,1},{3,2},{4,3},{5,4},{6,5},{7,6},{8,7},{9,8},{10,9},{11,1... | collective-permute-start | bytes 36872 | tf_op jit(solution)/shard_map/ppermute | solution.py:16
  150.0 54.6 %collective-permute-start.3 = (f32[3,4,256,1]{2,1,3,0:T(4,128)}, f32[3,4,256,1]{2,1,3,0:T(4,128)}, u32[]{:S(2)}, u32[]{:S(2)}) collective-permute-start(f32[3,4,256,1]{2,1,3,0:T(4,128)} %copy.70), channel_id=1, source_target_pairs={{0,1},{1,2},{2,3},{3,4},{4,5},{5,6},{6,7},{7,8},{8,9},{9,10},{10,1... | collective-permute-start | bytes 36872 | tf_op jit(solution)/shard_map/ppermute | solution.py:14
  202.1 4.8 %copy-start.7 = (f32[256]{0:T(256)S(1)}, f32[256]{0:T(256)}, u32[]{:S(2)}) copy-start(f32[256]{0:T(256)} %get-tuple-element.18) | copy-start | bytes 3076
  202.1 4.8 %copy-start.8 = (f32[256]{0:T(256)S(1)}, f32[256]{0:T(256)}, u32[]{:S(2)}) copy-start(f32[256]{0:T(256)} %get-tuple-element.19) | copy-start | bytes 3076
where the time goes:
time: 211 us; the launch traced here: 210 us
  blocking collectives  78.4 us (37%)
  local copies, waits for them, and re-layouts  67.4 us (32%)
  starting transfers between devices  31.8 us (15%)
  other arithmetic  31.7 us (15%)
    all_gather x1, blocking collectives, body(): lax.all_gather(records, 'azi', axis=1, tiled=True)  43.3 us
    all_gather x1, blocking collectives, body(): lax.all_gather(cell_ids, 'azi', axis=1, tiled=True)  35.1 us
    scatter-add x1, other arithmetic, body(): jnp.zeros_like(flat_field).at[:, flat_index].add(pushes)  25 us
    reshape x1, local copies, waits for them, and re-layouts, body(): jnp.zeros_like(flat_field).at[:, flat_index].add(pushes)  18.6 us
    unnamed x22, local copies, waits for them, and re-layouts  17.9 us
    ppermute x2, starting transfers between devices, with_halo(): lax.ppermute(head, axis, [((i + 1) % count, i) for i in range(count)])  16 us
    gather x1, local copies, waits for them, and re-layouts, body(): flat_field[:, flat_index].reshape(3, owners, slots)  16 us
    all_to_all x1, starting transfers between devices, body(): lax.all_to_all(updated, 'azi', split_axis=2, concat_axis=2, tiled=True)  8.68 us
  transfers between devices with their start and end apart: 5, of which 0 were waited for; matrix products, arithmetic and copies ran while one was open for 44% of the time, Pallas kernels for 0%

commit v1 on v0

v1 whole, which is shorter than its diff:
```python
import functools

import jax
import jax.numpy as jnp
from jax import lax
from jax.experimental import pallas as pl
from jax.experimental.pallas import tpu as pltpu
from jax.sharding import PartitionSpec as P

MESH = pl.DeviceIdType.MESH
F32, BF16, I32 = jnp.float32, jnp.bfloat16, jnp.int32
GROUP = 4


def iota(shape, dim):
    return lax.broadcasted_iota(I32, shape, dim)


def remote(src, dst, send, recv, to):
    return pltpu.make_async_remote_copy(src, dst, send, recv, device_id=to, device_id_type=MESH)


def column(row):
    return jnp.broadcast_to(row, (row.shape[1], row.shape[1])).T


def kernel(sizes, vel, mean, part_x, part_r, part_t, part_vel, part_rate, counts, out_v, out_p,
           field, mean_b, x_b, r_b, t_b, vel_b, rate_b, counts_b, msg, rec, back, home, planes, edge, edge_in,
           turned, hot, push, load_sem, plane_send, plane_recv, rec_send, rec_recv, back_send, back_recv, edge_send, edge_recv):
    ns, na = sizes
    _, _, nr, nt = field.shape
    rows = 2 * nr
    s, a = lax.axis_index("stream"), lax.axis_index("azi")
    right, left = (lax.rem(s + 1, ns), a), (lax.rem(s + ns - 1, ns), a)

    def ahead(i):
        return lax.rem(a + i, na)

    barrier = pltpu.get_barrier_semaphore()
    peers = [right, left] + [(s, ahead(i)) for i in range(1, na)]
    for peer in peers:
        pl.semaphore_signal(barrier, inc=1, device_id=peer, device_id_type=MESH)
    loads = [
        pltpu.make_async_copy(src, dst, load_sem.at[i])
        for i, (src, dst) in enumerate(
            [(part_x, x_b), (part_r, r_b), (part_t, t_b), (part_vel, vel_b), (part_rate, rate_b), (counts, counts_b), (mean, mean_b), (vel, field)]
        )
    ]
    for load in loads:
        load.start()
    for load in loads[:6]:
        load.wait()

    cnt = jnp.where(iota((na, na), 0) == iota((na, na), 1), counts_b[0].astype(F32), 0.0)
    cnt = jnp.sum(cnt, axis=1, keepdims=True)
    live = iota((na, nt), 1).astype(F32) < cnt
    for c in range(3):
        msg[:, c, :] = vel_b[0, 0, c]
    msg[:, 3, :] = jnp.where(live, rate_b[0, 0], 0.0)
    msg[:, 4, :] = (x_b[0, 0] * nr + r_b[0, 0]).astype(F32)
    msg[:, 5, :] = t_b[0, 0].astype(F32)
    msg[:, 6:8, :] = jnp.zeros((na, 2, nt), F32)

    loads[6].wait()
    loads[7].wait()
    pl.semaphore_wait(barrier, len(peers))
    sent = []
    for c in range(3):
        for d, to in ((0, right), (1, left)):
            cp = remote(field.at[c, 1 - d], planes.at[d, c], plane_send.at[d, c], plane_recv.at[d, c], to)
            cp.start()
            sent.append(cp)
    records = [None]
    for i in range(1, na):
        cp = remote(msg.at[ahead(i)], rec.at[i], rec_send.at[i], rec_recv.at[i], (s, ahead(i)))
        cp.start()
        records.append(cp)
    rec[0] = msg[a]

    edge[:, 3:8, :] = jnp.zeros((2, 5, rows), F32)
    for c in range(3):
        for p in range(2):
            for k in range(0, nr, nt):
                at = p * nr + k
                block = field[c, p, pl.ds(k, nt), :].T
                edge[0, c:c + 1, at:at + nt] = block[0:1]
                edge[1, c:c + 1, at:at + nt] = block[nt - 1:nt]
                high = block.astype(BF16)
                turned[c * nt:(c + 1) * nt, at:at + nt] = high
                turned[(3 + c) * nt:(4 + c) * nt, at:at + nt] = (block - high.astype(F32)).astype(BF16)
    for d, to in ((0, (s, ahead(1))), (1, (s, ahead(na - 1)))):
        cp = remote(edge.at[1 - d], edge_in.at[d], edge_send.at[d], edge_recv.at[d], to)
        cp.start()
        sent.append(cp)

    j = iota((nr, nt), 0)
    radius = 0.5 + 0.5 * (j.astype(F32) + 0.5) / nr
    h = 0.25 / (nr * radius)
    k = (0.75 / radius) * (0.75 / radius)
    flow = 0.15 * jnp.concatenate([column(mean_b[i:i + nt].reshape(1, nt)) for i in range(0, nr, nt)], axis=0)
    lane = iota((nr, nt), 1)
    own = 1.0 - 0.32 - 0.16 * k
    outer = jnp.where(j < nr - 1, 0.08 * (1.0 + h), 0.0)
    inner = jnp.where(j > 0, 0.08 * (1.0 - h), 0.0)
    after = jnp.where(lane < nt - 1, 0.08 * k, 0.0)
    before = jnp.where(lane > 0, 0.08 * k, 0.0)
    up, down = 0.08 - flow, 0.08 + flow
    for c in range(3):
        for p in range(2):
            u = field[c, p]
            new = u * own + outer * pltpu.roll(u, nr - 1, 0) + inner * pltpu.roll(u, 1, 0)
            new += after * pltpu.roll(u, nt - 1, 1) + before * pltpu.roll(u, 1, 1)
            out_v[c, p] = new + (up if p == 0 else down) * field[c, 1 - p]

    for g in range(0, na, GROUP):
        for i in range(g, g + GROUP):
            if i:
                records[i].wait_recv()
            row = rec[i, 4:5, :].astype(I32)
            hot[:, i * nt:(i + 1) * nt] = jnp.where(iota((rows, nt), 0) == row, 1.0, 0.0).astype(BF16)
        at = lax.dot_general(turned[...], hot[:, g * nt:(g + GROUP) * nt], (((1,), (0,)), ((), ())), preferred_element_type=F32)
        at = at[:3 * nt] + at[3 * nt:]
        for i in range(g, g + GROUP):
            here = iota((nt, nt), 0) == rec[i, 5:6, :].astype(I32)
            rate = 0.1 * rec[i, 3:4, :]
            for c in range(3):
                fluid = at[c * nt:(c + 1) * nt, (i - g) * nt:(i - g + 1) * nt]
                fluid = jnp.sum(jnp.where(here, fluid, 0.0), axis=0, keepdims=True)
                old = rec[i, c:c + 1, :]
                kick = rate * (fluid - old)
                back[i, c:c + 1, :] = old + kick
                kick = -0.5 * kick
                high = kick.astype(BF16).astype(F32)
                push[0, c * nt:(c + 1) * nt, i * nt:(i + 1) * nt] = jnp.where(here, high, 0.0).astype(BF16)
                push[1, c * nt:(c + 1) * nt, i * nt:(i + 1) * nt] = jnp.where(here, kick - high, 0.0).astype(BF16)
            if i:
                cp = remote(back.at[i], home.at[a], back_send.at[i], back_recv.at[i], (s, ahead(na - i)))
                cp.start()
                sent.append(cp)
            else:
                home[a] = back[0]

    contract = (((1,), (1,)), ((), ()))
    deposit = lax.dot_general(hot[...], push[0], contract, preferred_element_type=F32)
    deposit += lax.dot_general(hot[...], push[1], contract, preferred_element_type=F32)

    for cp in sent[6:8]:
        cp.wait_recv()
    lanes = lax.rem(iota((1, rows), 1), nr).astype(F32)
    radius = 0.5 + 0.5 * (lanes + 0.5) / nr
    k = 0.08 * (0.75 / radius) * (0.75 / radius)
    sides = jnp.concatenate([edge_in[0], edge_in[1]], axis=0) * k
    which, where = iota((16, 3 * nt), 0), iota((16, 3 * nt), 1)
    place = jnp.logical_or(where == which * nt, where == (which - 8) * nt + nt - 1)
    place = jnp.where(jnp.logical_and(place, lax.rem(which, 8) < 3), 1.0, 0.0)
    deposit += lax.dot_general(sides, place, (((0,), (0,)), ((), ())), preferred_element_type=F32, precision=lax.Precision.HIGHEST)

    for c in range(3):
        for p in range(2):
            sent[2 * c + p].wait_recv()
            new = out_v[c, p] + deposit[p * nr:(p + 1) * nr, c * nt:(c + 1) * nt]
            out_v[c, p] = new + (down if p == 0 else up) * planes[p, c]

    for i in range(1, na):
        records[i].wait_send()
    for cp in sent:
        cp.wait_send()
    for cp in sent[8:]:
        cp.wait_recv()
    for c in range(3):
        out_p[0, 0, c] = home[:, c, :]


def body(velocity, mean_flow, part_x, part_r, part_t, part_vel, part_rate, counts):
    ns, na = lax.axis_size("stream"), lax.axis_size("azi")
    _, _, nr, nt = velocity.shape
    rows = 2 * nr
    sem = pltpu.SemaphoreType.DMA
    part_vel = jnp.swapaxes(part_vel, 2, 3)
    inputs = (velocity, mean_flow, part_x, part_r, part_t, part_vel, part_rate, counts)
    inputs = tuple(pltpu.with_memory_space_constraint(x, pltpu.HBM) for x in inputs)
    staged = [pltpu.VMEM(x.shape, x.dtype) for x in inputs]
    new_velocity, new_vel = pl.pallas_call(
        functools.partial(kernel, (ns, na)),
        out_shape=(pltpu.VMEM(velocity.shape, F32), pltpu.VMEM(part_vel.shape, F32)),
        in_specs=[pl.BlockSpec(memory_space=pltpu.HBM)] * 8,
        out_specs=[pl.BlockSpec(memory_space=pltpu.VMEM)] * 2,
        scratch_shapes=staged
        + [
            pltpu.VMEM((na, 8, nt), F32),
            pltpu.VMEM((na, 8, nt), F32),
            pltpu.VMEM((na, 3, nt), F32),
            pltpu.VMEM((na, 3, nt), F32),
            pltpu.VMEM((2, 3, nr, nt), F32),
            pltpu.VMEM((2, 8, rows), F32),
            pltpu.VMEM((2, 8, rows), F32),
            pltpu.VMEM((6 * nt, rows), BF16),
            pltpu.VMEM((rows, na * nt), BF16),
            pltpu.VMEM((2, 3 * nt, na * nt), BF16),
            sem((8,)), sem((2, 3)), sem((2, 3)), sem((na,)), sem((na,)), sem((na,)), sem((na,)), sem((2,)), sem((2,)),
        ],
        compiler_params=pltpu.CompilerParams(collective_id=0, has_side_effects=True, vmem_limit_bytes=48 * 1024 * 1024),
        name="substep",
    )(*inputs)
    return new_velocity, jnp.swapaxes(new_vel, 2, 3)


def solution(mesh):
    in_specs = (
        P(None, "stream", None, "azi"),
        P(),
        P("stream", "azi", None, None),
        P("stream", "azi", None, None),
        P("stream", "azi", None, None),
        P("stream", "azi", None, None, None),
        P("stream", "azi", None, None),
        P("stream", "azi", None),
    )
    out_specs = (P(None, "stream", None, "azi"), P("stream", "azi", None, None, None))
    return jax.shard_map(body, mesh=mesh, in_specs=in_specs, out_specs=out_specs, check_vma=False)
```

time: 211 us -> 37.3 us (0.18)
  the two profiles are of different devices: /device:TPU:6 before, /device:TPU:2 now
where the time goes in v1:
time: 37.3 us; the launch traced here: 37.1 us
  Pallas kernels  35 us (94%)
  local copies, waits for them, and re-layouts  1.49 us (4%)
  between operations  0.64 us (2%)
    pallas_call x1, Pallas kernels, body(): pl.pallas_call(functools.partial(kernel, (ns, na)), out_shape=(pltpu.VMEM...  35 us
    unnamed x2, local copies, waits for them, and re-layouts  1.49 us

profile of v1, /device:TPU:2, one launch (start us, length us, event | category | flops | bytes accessed | tf_op | source)
XLA Modules:
  0.0 37.1 jit_solution(9514339639042899030)
XLA Ops:
  0.6 35.0 %substep.1 = (f32[3,2,256,128]{3,2,1,0:T(8,128)S(1)}, f32[1,1,3,16,128]{4,3,2,1,0:T(8,128)S(1)}) custom-call(f32[3,2,256,128]{3,2,1,0:T(8,128)} %vel.1, f32[256]{0:T(256)} %mean.1, s32[1,1,16,128]{3,2,1,0:T(8,128)} %part_x.1, s32[1,1,16,128]{3,2,1,0:T(8,128)} %part_r.1, s32[1,1,16,128]{3,2,1,0:T(8,128)} %part_t.1, f32[1,1,3,16,128]{4,3,2,1,0:T(8,128)} %bitcast.3, ...), custom_call_target="tpu_custom_call" | custom-call | tf_op jit(solution)/shard_map/substep/pallas_call | solution.py:183
  35.6 0.9 %copy.12 = f32[3,2,256,128]{3,2,1,0:T(8,128)} copy(f32[3,2,256,128]{3,2,1,0:T(8,128)S(1)} %get-tuple-element.6) | data formatting | bytes 1572864
  36.5 0.6 %copy.13 = f32[1,1,16,3,128]{4,2,3,1,0:T(8,128)} copy(f32[1,1,16,3,128]{4,2,3,1,0:T(8,128)S(1)} %bitcast.2) | data formatting | bytes 49152

commit v2 on v1

v2 whole, which is shorter than its diff:
```python
import functools

import jax
import jax.numpy as jnp
from jax import lax
from jax.experimental import pallas as pl
from jax.experimental.pallas import tpu as pltpu
from jax.sharding import PartitionSpec as P

MESH = pl.DeviceIdType.MESH
F32, BF16, I32 = jnp.float32, jnp.bfloat16, jnp.int32
GROUP, PARTS = 4, 4


def iota(shape, dim):
    return lax.broadcasted_iota(I32, shape, dim)


def remote(src, dst, send, recv, to):
    return pltpu.make_async_remote_copy(src, dst, send, recv, device_id=to, device_id_type=MESH)


def column(row):
    return jnp.broadcast_to(row, (row.shape[1], row.shape[1])).T


def kernel(sizes, vel, mean, part_x, part_r, part_t, part_vel, part_rate, counts, out_v, out_p,
           field, mean_b, x_b, r_b, t_b, vel_b, rate_b, counts_b, msg, rec, back, home, planes, edge, edge_in,
           turned, hot, push, load_sem, ready, near, go, passing, pass_send, pass_recv, plane_send, plane_recv, rec_send, rec_recv, back_send, back_recv, edge_send, edge_recv):
    ns, na = sizes
    _, _, nr, nt = field.shape
    rows, groups = 2 * nr, na // GROUP
    s, a = lax.axis_index("stream"), lax.axis_index("azi")
    right, left = lax.rem(s + 1, ns), lax.rem(s + ns - 1, ns)
    mine = a // GROUP
    half, part = ns // 2, nr // PARTS
    p, late = lax.rem(s, half), s >= half
    first, last = p == 0, p == half - 1
    over = lax.rem(s + half, ns)
    away = jnp.where(p < half // 2, p, half - 1 - p) // 2
    relay = jnp.logical_and(jnp.where(p < half // 2, p, half - 1 - p) == 2 * away, jnp.logical_and(away > 0, away < PARTS))
    upper = p >= half // 2

    def each(first, last, act):
        def step(i, carry):
            act(i)
            return carry

        lax.fori_loop(first, last, step, 0)

    def signal(sem, to):
        pl.semaphore_signal(sem, inc=1, device_id=to, device_id_type=MESH)

    barrier = pltpu.get_barrier_semaphore()
    each(a + 1, na, lambda i: signal(barrier, (s, i)))
    pl.when(right > s)(lambda: signal(barrier, (right, a)))
    pl.when(left > s)(lambda: signal(barrier, (left, a)))
    for n in range(1, PARTS):
        pl.when(first)(lambda: signal(barrier, (s + 2 * n, a)))
        pl.when(jnp.logical_and(first, s < half))(lambda: signal(barrier, (ns - 1 - 2 * n, a)))
        pl.when(jnp.logical_and(last, s < half))(lambda: signal(barrier, (half + 2 * n, a)))
    end = s - p + half - 1
    pl.when(jnp.logical_and(relay, s < half))(lambda: signal(barrier, (jnp.where(upper, half, ns - 1), a)))
    pl.when(jnp.logical_and(relay, upper))(lambda: signal(barrier, (end, a)))
    loads = [
        pltpu.make_async_copy(src, dst, load_sem.at[i])
        for i, (src, dst) in enumerate(
            [(part_x, x_b), (part_r, r_b), (part_t, t_b), (part_vel, vel_b), (part_rate, rate_b), (counts, counts_b), (mean, mean_b), (vel, field)]
        )
    ]
    for load in loads:
        load.start()
    earlier = a + jnp.where(left < s, 1, 0) + jnp.where(right < s, 1, 0)
    earlier += jnp.where(jnp.logical_and(late, jnp.logical_or(first, last)), PARTS - 1, 0) + jnp.where(last, PARTS - 1, 0)
    earlier += jnp.where(jnp.logical_and(relay, late), 1, 0) + jnp.where(jnp.logical_and(relay, jnp.logical_not(upper)), 1, 0)
    pl.when(earlier > 0)(lambda: pl.semaphore_wait(barrier, earlier))
    pl.when(left < s)(lambda: signal(near.at[0], (left, a)))
    pl.when(right < s)(lambda: signal(near.at[1], (right, a)))
    pl.when(jnp.logical_and(relay, late))(lambda: signal(near.at[jnp.where(upper, 1, 0)], (jnp.where(upper, 0, half - 1), a)))
    for n in range(1, PARTS):
        pl.when(last)(lambda: signal(go.at[0], (s - 2 * n, a)))

    def plane(d, n):
        at = pl.ds(n * part, part)
        to = (left if d else right, a)
        return remote(vel.at[:, 1 - d, at], planes.at[d, :, at], plane_send.at[d, n], plane_recv.at[d, n], to)

    def first_leg(d, n):
        at = pl.ds(n * part, part)
        to = (left - 2 * n if d else right + 2 * n, a)
        return remote(vel.at[:, 1 - d, at], passing, plane_send.at[d, n], pass_recv.at[0], to)

    def second_leg():
        at = pl.ds(pl.multiple_of(away * part, part), part)
        d = jnp.where(upper, 1, 0)
        to = (jnp.where(upper, end, s - p), a)
        return remote(passing, planes.at[d, :, at], pass_send.at[0], plane_recv.at[d, away], to)

    def send_planes(d):
        for n in range(PARTS):
            plane(d, n).start()

    def send_far(d):
        for n in reversed(range(PARTS)):
            (first_leg(d, n) if n else plane(d, n)).start()

    def pass_on():
        pl.when(upper)(lambda: pl.semaphore_wait(go.at[0], 1))
        first_leg(0, 1).wait_recv()
        second_leg().start()

    def record(i, src, dst, send, recv, slot):
        return remote(src.at[i], dst.at[slot], send.at[i], recv.at[slot], (s, i))

    def send_record(i):
        record(i, msg, rec, rec_send, rec_recv, a).start()

    def meet(i):
        pl.semaphore_wait(ready.at[i], 1)
        send_record(i)

    pl.when(jnp.logical_and(last, late))(lambda: send_far(0))
    pl.when(jnp.logical_and(first, late))(lambda: send_far(1))
    pl.when(jnp.logical_not(first))(lambda: send_planes(1))
    each(0, a, lambda i: signal(ready.at[a], (s, i)))

    for load in loads[:6]:
        load.wait()
    cnt = jnp.where(iota((na, na), 0) == iota((na, na), 1), counts_b[0].astype(F32), 0.0)
    cnt = jnp.sum(cnt, axis=1, keepdims=True)
    live = iota((na, nt), 1).astype(F32) < cnt
    for c in range(3):
        msg[:, c, :] = vel_b[0, 0, c]
    msg[:, 3, :] = jnp.where(live, rate_b[0, 0], 0.0)
    msg[:, 4, :] = (x_b[0, 0] * nr + r_b[0, 0]).astype(F32)
    msg[:, 5, :] = t_b[0, 0].astype(F32)
    msg[:, 6:8, :] = jnp.zeros((na, 2, nt), F32)
    each(0, a, send_record)
    each(a + 1, (mine + 1) * GROUP, meet)
    rec[a] = msg[a]

    @pl.when(jnp.logical_not(last))
    def _():
        pl.semaphore_wait(near.at[0], 1)
        send_planes(0)

    loads[6].wait()
    loads[7].wait()
    edge[:, 3:8, :] = jnp.zeros((2, 5, rows), F32)
    for c in range(3):
        for m in range(2):
            for k in range(0, nr, nt):
                at = m * nr + k
                block = field[c, m, pl.ds(k, nt), :].T
                edge[0, c:c + 1, at:at + nt] = block[0:1]
                edge[1, c:c + 1, at:at + nt] = block[nt - 1:nt]
                high = block.astype(BF16)
                turned[c * nt:(c + 1) * nt, at:at + nt] = high
                turned[(3 + c) * nt:(4 + c) * nt, at:at + nt] = (block - high.astype(F32)).astype(BF16)

    j = iota((nr, nt), 0)
    radius = 0.5 + 0.5 * (j.astype(F32) + 0.5) / nr
    h = 0.25 / (nr * radius)
    k = (0.75 / radius) * (0.75 / radius)
    flow = 0.15 * jnp.concatenate([column(mean_b[i:i + nt].reshape(1, nt)) for i in range(0, nr, nt)], axis=0)
    lane = iota((nr, nt), 1)
    own = 1.0 - 0.32 - 0.16 * k
    outer = jnp.where(j < nr - 1, 0.08 * (1.0 + h), 0.0)
    inner = jnp.where(j > 0, 0.08 * (1.0 - h), 0.0)
    after = jnp.where(lane < nt - 1, 0.08 * k, 0.0)
    before = jnp.where(lane > 0, 0.08 * k, 0.0)
    up, down = 0.08 - flow, 0.08 + flow
    for c in range(3):
        for m in range(2):
            u = field[c, m]
            new = u * own + outer * pltpu.roll(u, nr - 1, 0) + inner * pltpu.roll(u, 1, 0)
            new += after * pltpu.roll(u, nt - 1, 1) + before * pltpu.roll(u, 1, 1)
            out_v[c, m] = new + (up if m == 0 else down) * field[c, 1 - m]

    edges = [
        remote(edge.at[1 - d], edge_in.at[d], edge_send.at[d], edge_recv.at[d], (s, lax.rem(a + (1 if d == 0 else na - 1), na)))
        for d in range(2)
    ]
    for q in range(groups):
        later = mine + 1 + q
        pl.when(later < groups)(lambda: each(later * GROUP, (later + 1) * GROUP, meet))
        if q == groups - 2:
            for cp in edges:
                cp.start()
        start = jnp.where(q <= mine, mine - q, q) * GROUP
        for n in range(GROUP):
            i = start + n
            pl.when(i != a)(lambda: record(i, msg, rec, rec_send, rec_recv, i).wait_recv())
            row = rec[i, 4:5, :].astype(I32)
            at = (q * GROUP + n) * nt
            hot[:, at:at + nt] = jnp.where(iota((rows, nt), 0) == row, 1.0, 0.0).astype(BF16)
        at = q * GROUP * nt
        values = lax.dot_general(turned[...], hot[:, at:at + GROUP * nt], (((1,), (0,)), ((), ())), preferred_element_type=F32)
        values = values[:3 * nt] + values[3 * nt:]
        for n in range(GROUP):
            i, at = start + n, (q * GROUP + n) * nt
            here = iota((nt, nt), 0) == rec[i, 5:6, :].astype(I32)
            rate = 0.1 * rec[i, 3:4, :]
            for c in range(3):
                fluid = values[c * nt:(c + 1) * nt, n * nt:(n + 1) * nt]
                fluid = jnp.sum(jnp.where(here, fluid, 0.0), axis=0, keepdims=True)
                old = rec[i, c:c + 1, :]
                kick = rate * (fluid - old)
                back[i, c:c + 1, :] = old + kick
                kick = -0.5 * kick
                high = kick.astype(BF16).astype(F32)
                push[0, c * nt:(c + 1) * nt, at:at + nt] = jnp.where(here, high, 0.0).astype(BF16)
                push[1, c * nt:(c + 1) * nt, at:at + nt] = jnp.where(here, kick - high, 0.0).astype(BF16)
            pl.when(i != a)(lambda: record(i, back, home, back_send, back_recv, a).start())
    home[a] = back[a]

    for d, edge_of in ((0, last), (1, first)):
        @pl.when(jnp.logical_and(edge_of, s < half))
        def _():
            pl.semaphore_wait(near.at[d], PARTS)
            send_far(d)

    pl.when(relay)(pass_on)

    contract = (((1,), (1,)), ((), ()))
    deposit = lax.dot_general(hot[...], push[0], contract, preferred_element_type=F32)
    deposit += lax.dot_general(hot[...], push[1], contract, preferred_element_type=F32)

    for cp in edges:
        cp.wait_recv()
    lanes = lax.rem(iota((1, rows), 1), nr).astype(F32)
    radius = 0.5 + 0.5 * (lanes + 0.5) / nr
    k = 0.08 * (0.75 / radius) * (0.75 / radius)
    sides = jnp.concatenate([edge_in[0], edge_in[1]], axis=0) * k
    which, where = iota((16, 3 * nt), 0), iota((16, 3 * nt), 1)
    place = jnp.logical_or(where == which * nt, where == (which - 8) * nt + nt - 1)
    place = jnp.where(jnp.logical_and(place, lax.rem(which, 8) < 3), 1.0, 0.0)
    deposit += lax.dot_general(sides, place, (((0,), (0,)), ((), ())), preferred_element_type=F32, precision=lax.Precision.HIGHEST)

    for n in range(PARTS):
        for d in range(2):
            plane(d, n).wait_recv()
            for c in range(3):
                lo, hi = n * part, (n + 1) * part
                new = out_v[c, d, lo:hi] + deposit[d * nr + lo:d * nr + hi, c * nt:(c + 1) * nt]
                out_v[c, d, lo:hi] = new + (down if d == 0 else up)[lo:hi] * planes[d, c, lo:hi]

    def settle(i):
        record(i, msg, rec, rec_send, rec_recv, a).wait_send()
        record(i, back, home, back_send, back_recv, a).wait_send()
        record(i, back, home, back_send, back_recv, i).wait_recv()

    each(0, a, settle)
    each(a + 1, na, settle)
    for c in range(3):
        out_p[0, 0, c] = home[:, c, :]
    for d in range(2):
        edges[d].wait_send()
        for n in range(PARTS):
            plane(d, n).wait_send()
    pl.when(relay)(lambda: second_leg().wait_send())


def body(velocity, mean_flow, part_x, part_r, part_t, part_vel, part_rate, counts):
    ns, na = lax.axis_size("stream"), lax.axis_size("azi")
    _, _, nr, nt = velocity.shape
    rows = 2 * nr
    sem = pltpu.SemaphoreType.DMA
    part_vel = jnp.swapaxes(part_vel, 2, 3)
    inputs = (velocity, mean_flow, part_x, part_r, part_t, part_vel, part_rate, counts)
    inputs = tuple(pltpu.with_memory_space_constraint(x, pltpu.HBM) for x in inputs)
    staged = [pltpu.VMEM(x.shape, x.dtype) for x in inputs]
    new_velocity, new_vel = pl.pallas_call(
        functools.partial(kernel, (ns, na)),
        out_shape=(pltpu.VMEM(velocity.shape, F32), pltpu.VMEM(part_vel.shape, F32)),
        in_specs=[pl.BlockSpec(memory_space=pltpu.HBM)] * 8,
        out_specs=[pl.BlockSpec(memory_space=pltpu.VMEM)] * 2,
        scratch_shapes=staged
        + [
            pltpu.VMEM((na, 8, nt), F32),
            pltpu.VMEM((na, 8, nt), F32),
            pltpu.VMEM((na, 3, nt), F32),
            pltpu.VMEM((na, 3, nt), F32),
            pltpu.VMEM((2, 3, nr, nt), F32),
            pltpu.VMEM((2, 8, rows), F32),
            pltpu.VMEM((2, 8, rows), F32),
            pltpu.VMEM((6 * nt, rows), BF16),
            pltpu.VMEM((rows, na * nt), BF16),
            pltpu.VMEM((2, 3 * nt, na * nt), BF16),
            sem((8,)), pltpu.SemaphoreType.REGULAR((na,)), pltpu.SemaphoreType.REGULAR((2,)), pltpu.SemaphoreType.REGULAR((1,)),
            pltpu.VMEM((3, nr // PARTS, nt), F32), sem((1,)), sem((1,)), sem((2, PARTS)), sem((2, PARTS)), sem((na,)), sem((na,)), sem((na,)), sem((na,)), sem((2,)), sem((2,)),
        ],
        compiler_params=pltpu.CompilerParams(collective_id=0, has_side_effects=True, vmem_limit_bytes=48 * 1024 * 1024),
        name="substep",
    )(*inputs)
    return new_velocity, jnp.swapaxes(new_vel, 2, 3)


def solution(mesh):
    in_specs = (
        P(None, "stream", None, "azi"),
        P(),
        P("stream", "azi", None, None),
        P("stream", "azi", None, None),
        P("stream", "azi", None, None),
        P("stream", "azi", None, None, None),
        P("stream", "azi", None, None),
        P("stream", "azi", None),
    )
    out_specs = (P(None, "stream", None, "azi"), P("stream", "azi", None, None, None))
    return jax.shard_map(body, mesh=mesh, in_specs=in_specs, out_specs=out_specs, check_vma=False)
```

time: 37.3 us -> 29.3 us (0.79)
  the two profiles are of different devices: /device:TPU:2 before, /device:TPU:6 now
where the time goes in v2:
time: 29.3 us; the launch traced here: 29.1 us
  Pallas kernels  27 us (92%)
  local copies, waits for them, and re-layouts  1.49 us (5%)
  between operations  0.64 us (2%)
    pallas_call x1, Pallas kernels, body(): pl.pallas_call(functools.partial(kernel, (ns, na)), out_shape=(pltpu.VMEM...  27 us
    unnamed x2, local copies, waits for them, and re-layouts  1.49 us

profile of v2, /device:TPU:6, one launch (start us, length us, event | category | flops | bytes accessed | tf_op | source)
XLA Modules:
  0.0 29.1 jit_solution(1548713084049416152)
XLA Ops:
  0.6 27.0 %substep.1 = (f32[3,2,256,128]{3,2,1,0:T(8,128)S(1)}, f32[1,1,3,16,128]{4,3,2,1,0:T(8,128)S(1)}) custom-call(f32[3,2,256,128]{3,2,1,0:T(8,128)} %vel.1, f32[256]{0:T(256)} %mean.1, s32[1,1,16,128]{3,2,1,0:T(8,128)} %part_x.1, s32[1,1,16,128]{3,2,1,0:T(8,128)} %part_r.1, s32[1,1,16,128]{3,2,1,0:T(8,128)} %part_t.1, f32[1,1,3,16,128]{4,3,2,1,0:T(8,128)} %bitcast.3, ...), custom_call_target="tpu_custom_call" | custom-call | tf_op jit(solution)/shard_map/substep/pallas_call | solution.py:273
  27.6 0.9 %copy.12 = f32[3,2,256,128]{3,2,1,0:T(8,128)} copy(f32[3,2,256,128]{3,2,1,0:T(8,128)S(1)} %get-tuple-element.6) | data formatting | bytes 1572864
  28.5 0.6 %copy.13 = f32[1,1,16,3,128]{4,2,3,1,0:T(8,128)} copy(f32[1,1,16,3,128]{4,2,3,1,0:T(8,128)S(1)} %bitcast.2) | data formatting | bytes 49152

commit v3 on v2

--- a/solution.py
+++ b/solution.py
@@ -9,7 +9,7 @@
 
 MESH = pl.DeviceIdType.MESH
 F32, BF16, I32 = jnp.float32, jnp.bfloat16, jnp.int32
-GROUP, PARTS = 4, 4
+GROUP, PARTS, RELAYS = 4, 4, 2
 
 
 def iota(shape, dim):
@@ -38,7 +38,7 @@
     first, last = p == 0, p == half - 1
     over = lax.rem(s + half, ns)
     away = jnp.where(p < half // 2, p, half - 1 - p) // 2
-    relay = jnp.logical_and(jnp.where(p < half // 2, p, half - 1 - p) == 2 * away, jnp.logical_and(away > 0, away < PARTS))
+    relay = jnp.logical_and(jnp.where(p < half // 2, p, half - 1 - p) == 2 * away, jnp.logical_and(away > 0, away <= RELAYS))
     upper = p >= half // 2
 
     def each(first, last, act):
@@ -55,7 +55,7 @@
     each(a + 1, na, lambda i: signal(barrier, (s, i)))
     pl.when(right > s)(lambda: signal(barrier, (right, a)))
     pl.when(left > s)(lambda: signal(barrier, (left, a)))
-    for n in range(1, PARTS):
+    for n in range(1, RELAYS + 1):
         pl.when(first)(lambda: signal(barrier, (s + 2 * n, a)))
         pl.when(jnp.logical_and(first, s < half))(lambda: signal(barrier, (ns - 1 - 2 * n, a)))
         pl.when(jnp.logical_and(last, s < half))(lambda: signal(barrier, (half + 2 * n, a)))
@@ -71,13 +71,13 @@
     for load in loads:
         load.start()
     earlier = a + jnp.where(left < s, 1, 0) + jnp.where(right < s, 1, 0)
-    earlier += jnp.where(jnp.logical_and(late, jnp.logical_or(first, last)), PARTS - 1, 0) + jnp.where(last, PARTS - 1, 0)
+    earlier += jnp.where(jnp.logical_and(late, jnp.logical_or(first, last)), RELAYS, 0) + jnp.where(last, RELAYS, 0)
     earlier += jnp.where(jnp.logical_and(relay, late), 1, 0) + jnp.where(jnp.logical_and(relay, jnp.logical_not(upper)), 1, 0)
     pl.when(earlier > 0)(lambda: pl.semaphore_wait(barrier, earlier))
     pl.when(left < s)(lambda: signal(near.at[0], (left, a)))
     pl.when(right < s)(lambda: signal(near.at[1], (right, a)))
     pl.when(jnp.logical_and(relay, late))(lambda: signal(near.at[jnp.where(upper, 1, 0)], (jnp.where(upper, 0, half - 1), a)))
-    for n in range(1, PARTS):
+    for n in range(1, RELAYS + 1):
         pl.when(last)(lambda: signal(go.at[0], (s - 2 * n, a)))
 
     def plane(d, n):
@@ -86,23 +86,28 @@
         return remote(vel.at[:, 1 - d, at], planes.at[d, :, at], plane_send.at[d, n], plane_recv.at[d, n], to)
 
     def first_leg(d, n):
-        at = pl.ds(n * part, part)
+        at = pl.ds((PARTS - n) * part, part)
         to = (left - 2 * n if d else right + 2 * n, a)
-        return remote(vel.at[:, 1 - d, at], passing, plane_send.at[d, n], pass_recv.at[0], to)
+        return remote(vel.at[:, 1 - d, at], passing, plane_send.at[d, PARTS - n], pass_recv.at[0], to)
 
     def second_leg():
-        at = pl.ds(pl.multiple_of(away * part, part), part)
+        n = PARTS - away
+        at = pl.ds(pl.multiple_of(n * part, part), part)
         d = jnp.where(upper, 1, 0)
         to = (jnp.where(upper, end, s - p), a)
-        return remote(passing, planes.at[d, :, at], pass_send.at[0], plane_recv.at[d, away], to)
+        return remote(passing, planes.at[d, :, at], pass_send.at[0], plane_recv.at[d, n], to)
 
     def send_planes(d):
         for n in range(PARTS):
             plane(d, n).start()
 
     def send_far(d):
-        for n in reversed(range(PARTS)):
-            (first_leg(d, n) if n else plane(d, n)).start()
+        for n in reversed(range(1, RELAYS + 1)):
+            first_leg(d, n).start()
+
+    def send_rest(d):
+        for n in range(PARTS - RELAYS):
+            plane(d, n).start()
 
     def pass_on():
         pl.when(upper)(lambda: pl.semaphore_wait(go.at[0], 1))
@@ -121,7 +126,6 @@
 
     pl.when(jnp.logical_and(last, late))(lambda: send_far(0))
     pl.when(jnp.logical_and(first, late))(lambda: send_far(1))
-    pl.when(jnp.logical_not(first))(lambda: send_planes(1))
     each(0, a, lambda i: signal(ready.at[a], (s, i)))
 
     for load in loads[:6]:
@@ -136,13 +140,19 @@
     msg[:, 5, :] = t_b[0, 0].astype(F32)
     msg[:, 6:8, :] = jnp.zeros((na, 2, nt), F32)
     each(0, a, send_record)
+    pl.when(jnp.logical_and(last, late))(lambda: send_rest(0))
+    pl.when(jnp.logical_and(first, late))(lambda: send_rest(1))
     each(a + 1, (mine + 1) * GROUP, meet)
     rec[a] = msg[a]
 
-    @pl.when(jnp.logical_not(last))
-    def _():
-        pl.semaphore_wait(near.at[0], 1)
-        send_planes(0)
+    def send_near():
+        pl.when(jnp.logical_not(first))(lambda: send_planes(1))
+
+        @pl.when(jnp.logical_not(last))
+        def _():
+            pl.semaphore_wait(near.at[0], 1)
+            send_planes(0)
+
 
     loads[6].wait()
     loads[7].wait()
@@ -181,12 +191,19 @@
         remote(edge.at[1 - d], edge_in.at[d], edge_send.at[d], edge_recv.at[d], (s, lax.rem(a + (1 if d == 0 else na - 1), na)))
         for d in range(2)
     ]
+    send_near()
     for q in range(groups):
         later = mine + 1 + q
         pl.when(later < groups)(lambda: each(later * GROUP, (later + 1) * GROUP, meet))
         if q == groups - 2:
             for cp in edges:
                 cp.start()
+        if q == groups - 1:
+            for d, edge_of in ((0, last), (1, first)):
+                @pl.when(jnp.logical_and(edge_of, s < half))
+                def _():
+                    pl.semaphore_wait(near.at[d], RELAYS + 1)
+                    send_far(d)
         start = jnp.where(q <= mine, mine - q, q) * GROUP
         for n in range(GROUP):
             i = start + n
@@ -214,18 +231,14 @@
             pl.when(i != a)(lambda: record(i, back, home, back_send, back_recv, a).start())
     home[a] = back[a]
 
-    for d, edge_of in ((0, last), (1, first)):
-        @pl.when(jnp.logical_and(edge_of, s < half))
-        def _():
-            pl.semaphore_wait(near.at[d], PARTS)
-            send_far(d)
-
-    pl.when(relay)(pass_on)
 
     contract = (((1,), (1,)), ((), ()))
     deposit = lax.dot_general(hot[...], push[0], contract, preferred_element_type=F32)
     deposit += lax.dot_general(hot[...], push[1], contract, preferred_element_type=F32)
 
+    pl.when(relay)(pass_on)
+    pl.when(jnp.logical_and(last, s < half))(lambda: send_rest(0))
+    pl.when(jnp.logical_and(first, s < half))(lambda: send_rest(1))
     for cp in edges:
         cp.wait_recv()
     lanes = lax.rem(iota((1, rows), 1), nr).astype(F32)
@@ -259,6 +272,15 @@
         for n in range(PARTS):
             plane(d, n).wait_send()
     pl.when(relay)(lambda: second_leg().wait_send())
+
+
+def store(velocity, part_vel, out_v, out_p, sems):
+    copies = [pltpu.make_async_copy(velocity.at[c], out_v.at[c], sems.at[c]) for c in range(3)]
+    copies.append(pltpu.make_async_copy(part_vel, out_p, sems.at[3]))
+    for copy in copies:
+        copy.start()
+    for copy in copies:
+        copy.wait()
 
 
 def body(velocity, mean_flow, part_x, part_r, part_t, part_vel, part_rate, counts):
@@ -293,6 +315,15 @@
         compiler_params=pltpu.CompilerParams(collective_id=0, has_side_effects=True, vmem_limit_bytes=48 * 1024 * 1024),
         name="substep",
     )(*inputs)
+    done = tuple(pltpu.with_memory_space_constraint(x, pltpu.VMEM) for x in (new_velocity, new_vel))
+    new_velocity, new_vel = pl.pallas_call(
+        store,
+        out_shape=tuple(pltpu.HBM(x.shape, x.dtype) for x in done),
+        in_specs=[pl.BlockSpec(memory_space=pltpu.VMEM)] * 2,
+        out_specs=[pl.BlockSpec(memory_space=pltpu.HBM)] * 2,
+        scratch_shapes=[sem((4,))],
+        name="store",
+    )(*done)
     return new_velocity, jnp.swapaxes(new_vel, 2, 3)
 
 

time: 29.3 us -> 27.2 us (0.928)
  local copies, waits for them, and re-layouts: 1.49 us -> 0 us
  Pallas kernels: 27 us -> 26.4 us
    unnamed x2 -> x0, local copies, waits for them, and re-layouts: 1.49 us -> none
    pallas_call x1, Pallas kernels: 27 us -> 25.5 us  [body(): pl.pallas_call(functools.partial(kernel, (ns, na)), out_shape=(pltpu.VMEM...]
    pallas_call x0 -> x1, Pallas kernels: none -> 0.91 us  [body(): pl.pallas_call(store, out_shape=tuple((pltpu.HBM(x.shape, x.dtype) for x...]
where the time goes in v3:
time: 27.2 us; the launch traced here: 27.1 us
  Pallas kernels  26.4 us (97%)
  between operations  0.64 us (2%)
    pallas_call x1, Pallas kernels, body(): pl.pallas_call(functools.partial(kernel, (ns, na)), out_shape=(pltpu.VMEM...  25.5 us
    pallas_call x1, Pallas kernels, body(): pl.pallas_call(store, out_shape=tuple((pltpu.HBM(x.shape, x.dtype) for x...  0.91 us

profile of v3, /device:TPU:6, one launch (start us, length us, event | category | flops | bytes accessed | tf_op | source)
XLA Modules:
  0.0 27.1 jit_solution(9479769490913500839)
XLA Ops:
  0.6 25.5 %substep.1 = (f32[3,2,256,128]{3,2,1,0:T(8,128)S(1)}, f32[1,1,3,16,128]{4,3,2,1,0:T(8,128)S(1)}) custom-call(f32[3,2,256,128]{3,2,1,0:T(8,128)} %vel.1, f32[256]{0:T(256)} %mean.1, s32[1,1,16,128]{3,2,1,0:T(8,128)} %part_x.1, s32[1,1,16,128]{3,2,1,0:T(8,128)} %part_r.1, s32[1,1,16,128]{3,2,1,0:T(8,128)} %part_t.1, f32[1,1,3,16,128]{4,3,2,1,0:T(8,128)} %bitcast.2, ...), custom_call_target="tpu_custom_call" | custom-call | tf_op jit(solution)/shard_map/substep/pallas_call | solution.py:295
  26.2 0.9 %store.1 = (f32[3,2,256,128]{3,2,1,0:T(8,128)}, f32[1,1,3,16,128]{4,3,2,1,0:T(8,128)}) custom-call(f32[3,2,256,128]{3,2,1,0:T(8,128)S(1)} %get-tuple-element.6.velocity, f32[1,1,3,16,128]{4,3,2,1,0:T(8,128)S(1)} %get-tuple-element.7.part_vel), custom_call_target="tpu_custom_call" | custom-call | tf_op jit(solution)/shard_map/store/pallas_call | solution.py:319

commit v4 on v3

--- a/solution.py
+++ b/solution.py
@@ -26,13 +26,12 @@
 
 def kernel(sizes, vel, mean, part_x, part_r, part_t, part_vel, part_rate, counts, out_v, out_p,
            field, mean_b, x_b, r_b, t_b, vel_b, rate_b, counts_b, msg, rec, back, home, planes, edge, edge_in,
-           turned, hot, push, load_sem, ready, near, go, passing, pass_send, pass_recv, plane_send, plane_recv, rec_send, rec_recv, back_send, back_recv, edge_send, edge_recv):
+           turned, hot, push, load_sem, ready, near, passing, pass_send, pass_recv, plane_send, plane_recv, rec_send, rec_recv, back_send, back_recv, edge_send, edge_recv):
     ns, na = sizes
     _, _, nr, nt = field.shape
     rows, groups = 2 * nr, na // GROUP
     s, a = lax.axis_index("stream"), lax.axis_index("azi")
     right, left = lax.rem(s + 1, ns), lax.rem(s + ns - 1, ns)
-    mine = a // GROUP
     half, part = ns // 2, nr // PARTS
     p, late = lax.rem(s, half), s >= half
     first, last = p == 0, p == half - 1
@@ -41,6 +40,19 @@
     relay = jnp.logical_and(jnp.where(p < half // 2, p, half - 1 - p) == 2 * away, jnp.logical_and(away > 0, away <= RELAYS))
     upper = p >= half // 2
 
+    shift = jnp.where(s == 0, 1, 0)
+    mine = lax.rem(a + na - shift, na) // GROUP
+
+    def peer(i):
+        return lax.rem(i + shift, na)
+
+    def rank(t):
+        q = lax.rem(t, half)
+        return (t // half) * ns + jnp.where(q < half // 2, 2 * q, 2 * (half - 1 - q) + 1)
+
+    order = lax.rem(a + na - shift, na)
+    left_first, right_first = rank(left) < rank(s), rank(right) < rank(s)
+
     def each(first, last, act):
         def step(i, carry):
             act(i)
@@ -52,16 +64,16 @@
         pl.semaphore_signal(sem, inc=1, device_id=to, device_id_type=MESH)
 
     barrier = pltpu.get_barrier_semaphore()
-    each(a + 1, na, lambda i: signal(barrier, (s, i)))
-    pl.when(right > s)(lambda: signal(barrier, (right, a)))
-    pl.when(left > s)(lambda: signal(barrier, (left, a)))
+    each(order + 1, na, lambda i: signal(barrier, (s, peer(i))))
+    pl.when(jnp.logical_not(right_first))(lambda: signal(barrier, (right, a)))
+    pl.when(jnp.logical_not(left_first))(lambda: signal(barrier, (left, a)))
     for n in range(1, RELAYS + 1):
         pl.when(first)(lambda: signal(barrier, (s + 2 * n, a)))
+        pl.when(last)(lambda: signal(barrier, (s - 2 * n, a)))
         pl.when(jnp.logical_and(first, s < half))(lambda: signal(barrier, (ns - 1 - 2 * n, a)))
         pl.when(jnp.logical_and(last, s < half))(lambda: signal(barrier, (half + 2 * n, a)))
     end = s - p + half - 1
     pl.when(jnp.logical_and(relay, s < half))(lambda: signal(barrier, (jnp.where(upper, half, ns - 1), a)))
-    pl.when(jnp.logical_and(relay, upper))(lambda: signal(barrier, (end, a)))
     loads = [
         pltpu.make_async_copy(src, dst, load_sem.at[i])
         for i, (src, dst) in enumerate(
@@ -70,15 +82,13 @@
     ]
     for load in loads:
         load.start()
-    earlier = a + jnp.where(left < s, 1, 0) + jnp.where(right < s, 1, 0)
-    earlier += jnp.where(jnp.logical_and(late, jnp.logical_or(first, last)), RELAYS, 0) + jnp.where(last, RELAYS, 0)
-    earlier += jnp.where(jnp.logical_and(relay, late), 1, 0) + jnp.where(jnp.logical_and(relay, jnp.logical_not(upper)), 1, 0)
+    earlier = order + jnp.where(left_first, 1, 0) + jnp.where(right_first, 1, 0)
+    earlier += jnp.where(jnp.logical_and(late, jnp.logical_or(first, last)), RELAYS, 0)
+    earlier += jnp.where(jnp.logical_and(relay, late), 1, 0) + jnp.where(relay, 1, 0)
     pl.when(earlier > 0)(lambda: pl.semaphore_wait(barrier, earlier))
-    pl.when(left < s)(lambda: signal(near.at[0], (left, a)))
-    pl.when(right < s)(lambda: signal(near.at[1], (right, a)))
+    pl.when(left_first)(lambda: signal(near.at[0], (left, a)))
+    pl.when(right_first)(lambda: signal(near.at[1], (right, a)))
     pl.when(jnp.logical_and(relay, late))(lambda: signal(near.at[jnp.where(upper, 1, 0)], (jnp.where(upper, 0, half - 1), a)))
-    for n in range(1, RELAYS + 1):
-        pl.when(last)(lambda: signal(go.at[0], (s - 2 * n, a)))
 
     def plane(d, n):
         at = pl.ds(n * part, part)
@@ -110,12 +120,13 @@
             plane(d, n).start()
 
     def pass_on():
-        pl.when(upper)(lambda: pl.semaphore_wait(go.at[0], 1))
         first_leg(0, 1).wait_recv()
         second_leg().start()
 
     def record(i, src, dst, send, recv, slot):
-        return remote(src.at[i], dst.at[slot], send.at[i], recv.at[slot], (s, i))
+        count = 6 if src is msg else 3
+        at = pl.ds(0, count)
+        return remote(src.at[i, at], dst.at[slot, at], send.at[i], recv.at[slot], (s, i))
 
     def send_record(i):
         record(i, msg, rec, rec_send, rec_recv, a).start()
@@ -126,7 +137,9 @@
 
     pl.when(jnp.logical_and(last, late))(lambda: send_far(0))
     pl.when(jnp.logical_and(first, late))(lambda: send_far(1))
-    each(0, a, lambda i: signal(ready.at[a], (s, i)))
+    pl.when(jnp.logical_and(last, late))(lambda: send_rest(0))
+    pl.when(jnp.logical_and(first, late))(lambda: send_rest(1))
+    each(0, order, lambda i: signal(ready.at[a], (s, peer(i))))
 
     for load in loads[:6]:
         load.wait()
@@ -138,20 +151,14 @@
     msg[:, 3, :] = jnp.where(live, rate_b[0, 0], 0.0)
     msg[:, 4, :] = (x_b[0, 0] * nr + r_b[0, 0]).astype(F32)
     msg[:, 5, :] = t_b[0, 0].astype(F32)
-    msg[:, 6:8, :] = jnp.zeros((na, 2, nt), F32)
-    each(0, a, send_record)
-    pl.when(jnp.logical_and(last, late))(lambda: send_rest(0))
-    pl.when(jnp.logical_and(first, late))(lambda: send_rest(1))
-    each(a + 1, (mine + 1) * GROUP, meet)
+    each(0, order, lambda i: send_record(peer(i)))
+    each(order + 1, (mine + 1) * GROUP, lambda i: meet(peer(i)))
     rec[a] = msg[a]
 
     def send_near():
-        pl.when(jnp.logical_not(first))(lambda: send_planes(1))
-
-        @pl.when(jnp.logical_not(last))
-        def _():
-            pl.semaphore_wait(near.at[0], 1)
-            send_planes(0)
+        for d, far, ahead in ((1, first, left_first), (0, last, right_first)):
+            pl.when(jnp.logical_not(jnp.logical_or(far, ahead)))(lambda: pl.semaphore_wait(near.at[d], 1))
+            pl.when(jnp.logical_not(far))(lambda: send_planes(d))
 
 
     loads[6].wait()
@@ -194,19 +201,20 @@
     send_near()
     for q in range(groups):
         later = mine + 1 + q
-        pl.when(later < groups)(lambda: each(later * GROUP, (later + 1) * GROUP, meet))
+        pl.when(later < groups)(lambda: each(later * GROUP, (later + 1) * GROUP, lambda i: meet(peer(i))))
         if q == groups - 2:
             for cp in edges:
                 cp.start()
-        if q == groups - 1:
+        if q == groups - 2:
             for d, edge_of in ((0, last), (1, first)):
                 @pl.when(jnp.logical_and(edge_of, s < half))
                 def _():
                     pl.semaphore_wait(near.at[d], RELAYS + 1)
                     send_far(d)
+                    send_rest(d)
         start = jnp.where(q <= mine, mine - q, q) * GROUP
         for n in range(GROUP):
-            i = start + n
+            i = peer(start + n)
             pl.when(i != a)(lambda: record(i, msg, rec, rec_send, rec_recv, i).wait_recv())
             row = rec[i, 4:5, :].astype(I32)
             at = (q * GROUP + n) * nt
@@ -215,7 +223,7 @@
         values = lax.dot_general(turned[...], hot[:, at:at + GROUP * nt], (((1,), (0,)), ((), ())), preferred_element_type=F32)
         values = values[:3 * nt] + values[3 * nt:]
         for n in range(GROUP):
-            i, at = start + n, (q * GROUP + n) * nt
+            i, at = peer(start + n), (q * GROUP + n) * nt
             here = iota((nt, nt), 0) == rec[i, 5:6, :].astype(I32)
             rate = 0.1 * rec[i, 3:4, :]
             for c in range(3):
@@ -230,15 +238,14 @@
                 push[1, c * nt:(c + 1) * nt, at:at + nt] = jnp.where(here, kick - high, 0.0).astype(BF16)
             pl.when(i != a)(lambda: record(i, back, home, back_send, back_recv, a).start())
     home[a] = back[a]
+    pl.when(jnp.logical_and(relay, late))(pass_on)
 
 
     contract = (((1,), (1,)), ((), ()))
     deposit = lax.dot_general(hot[...], push[0], contract, preferred_element_type=F32)
     deposit += lax.dot_general(hot[...], push[1], contract, preferred_element_type=F32)
 
-    pl.when(relay)(pass_on)
-    pl.when(jnp.logical_and(last, s < half))(lambda: send_rest(0))
-    pl.when(jnp.logical_and(first, s < half))(lambda: send_rest(1))
+    pl.when(jnp.logical_and(relay, jnp.logical_not(late)))(pass_on)
     for cp in edges:
         cp.wait_recv()
     lanes = lax.rem(iota((1, rows), 1), nr).astype(F32)
@@ -250,6 +257,15 @@
     place = jnp.where(jnp.logical_and(place, lax.rem(which, 8) < 3), 1.0, 0.0)
     deposit += lax.dot_general(sides, place, (((0,), (0,)), ((), ())), preferred_element_type=F32, precision=lax.Precision.HIGHEST)
 
+    def settle(i):
+        record(i, msg, rec, rec_send, rec_recv, a).wait_send()
+        record(i, back, home, back_send, back_recv, a).wait_send()
+        record(i, back, home, back_send, back_recv, i).wait_recv()
+
+    each(0, a, settle)
+    each(a + 1, na, settle)
+    for c in range(3):
+        out_p[0, 0, c] = home[:, c, :]
     for n in range(PARTS):
         for d in range(2):
             plane(d, n).wait_recv()
@@ -258,15 +274,6 @@
                 new = out_v[c, d, lo:hi] + deposit[d * nr + lo:d * nr + hi, c * nt:(c + 1) * nt]
                 out_v[c, d, lo:hi] = new + (down if d == 0 else up)[lo:hi] * planes[d, c, lo:hi]
 
-    def settle(i):
-        record(i, msg, rec, rec_send, rec_recv, a).wait_send()
-        record(i, back, home, back_send, back_recv, a).wait_send()
-        record(i, back, home, back_send, back_recv, i).wait_recv()
-
-    each(0, a, settle)
-    each(a + 1, na, settle)
-    for c in range(3):
-        out_p[0, 0, c] = home[:, c, :]
     for d in range(2):
         edges[d].wait_send()
         for n in range(PARTS):
@@ -309,7 +316,7 @@
             pltpu.VMEM((6 * nt, rows), BF16),
             pltpu.VMEM((rows, na * nt), BF16),
             pltpu.VMEM((2, 3 * nt, na * nt), BF16),
-            sem((8,)), pltpu.SemaphoreType.REGULAR((na,)), pltpu.SemaphoreType.REGULAR((2,)), pltpu.SemaphoreType.REGULAR((1,)),
+            sem((8,)), pltpu.SemaphoreType.REGULAR((na,)), pltpu.SemaphoreType.REGULAR((2,)),
             pltpu.VMEM((3, nr // PARTS, nt), F32), sem((1,)), sem((1,)), sem((2, PARTS)), sem((2, PARTS)), sem((na,)), sem((na,)), sem((na,)), sem((na,)), sem((2,)), sem((2,)),
         ],
         compiler_params=pltpu.CompilerParams(collective_id=0, has_side_effects=True, vmem_limit_bytes=48 * 1024 * 1024),

time: 27.2 us -> 27 us (level)
  the two profiles are of different devices: /device:TPU:6 before, /device:TPU:256 now
where the time goes in v4:
time: 27 us; the launch traced here: 26.8 us
  Pallas kernels  26.2 us (97%)
  between operations  0.64 us (2%)
    pallas_call x1, Pallas kernels, body(): pl.pallas_call(functools.partial(kernel, (ns, na)), out_shape=(pltpu.VMEM...  25.3 us
    pallas_call x1, Pallas kernels, body(): pl.pallas_call(store, out_shape=tuple((pltpu.HBM(x.shape, x.dtype) for x...  0.91 us

profile of v4, /device:TPU:256, one launch (start us, length us, event | category | flops | bytes accessed | tf_op | source)
XLA Modules:
  0.0 26.8 jit_solution(13490905427287456682)
XLA Ops:
  0.6 25.3 %substep.1 = (f32[3,2,256,128]{3,2,1,0:T(8,128)S(1)}, f32[1,1,3,16,128]{4,3,2,1,0:T(8,128)S(1)}) custom-call(f32[3,2,256,128]{3,2,1,0:T(8,128)} %vel.1, f32[256]{0:T(256)} %mean.1, s32[1,1,16,128]{3,2,1,0:T(8,128)} %part_x.1, s32[1,1,16,128]{3,2,1,0:T(8,128)} %part_r.1, s32[1,1,16,128]{3,2,1,0:T(8,128)} %part_t.1, f32[1,1,3,16,128]{4,3,2,1,0:T(8,128)} %bitcast.2, ...), custom_call_target="tpu_custom_call" | custom-call | tf_op jit(solution)/shard_map/substep/pallas_call | solution.py:302
  25.9 0.9 %store.1 = (f32[3,2,256,128]{3,2,1,0:T(8,128)}, f32[1,1,3,16,128]{4,3,2,1,0:T(8,128)}) custom-call(f32[3,2,256,128]{3,2,1,0:T(8,128)S(1)} %get-tuple-element.6.velocity, f32[1,1,3,16,128]{4,3,2,1,0:T(8,128)S(1)} %get-tuple-element.7.part_vel), custom_call_target="tpu_custom_call" | custom-call | tf_op jit(solution)/shard_map/store/pallas_call | solution.py:326

commit v5 on v4

--- a/solution.py
+++ b/solution.py
@@ -198,7 +198,6 @@
         remote(edge.at[1 - d], edge_in.at[d], edge_send.at[d], edge_recv.at[d], (s, lax.rem(a + (1 if d == 0 else na - 1), na)))
         for d in range(2)
     ]
-    send_near()
     for q in range(groups):
         later = mine + 1 + q
         pl.when(later < groups)(lambda: each(later * GROUP, (later + 1) * GROUP, lambda i: meet(peer(i))))
@@ -212,6 +211,8 @@
                     pl.semaphore_wait(near.at[d], RELAYS + 1)
                     send_far(d)
                     send_rest(d)
+        if q == 1:
+            send_near()
         start = jnp.where(q <= mine, mine - q, q) * GROUP
         for n in range(GROUP):
             i = peer(start + n)
@@ -282,8 +283,8 @@
 
 
 def store(velocity, part_vel, out_v, out_p, sems):
-    copies = [pltpu.make_async_copy(velocity.at[c], out_v.at[c], sems.at[c]) for c in range(3)]
-    copies.append(pltpu.make_async_copy(part_vel, out_p, sems.at[3]))
+    copies = [pltpu.make_async_copy(velocity.at[i // 2, i % 2], out_v.at[i // 2, i % 2], sems.at[i]) for i in range(6)]
+    copies.append(pltpu.make_async_copy(part_vel, out_p, sems.at[6]))
     for copy in copies:
         copy.start()
     for copy in copies:
@@ -328,7 +329,7 @@
         out_shape=tuple(pltpu.HBM(x.shape, x.dtype) for x in done),
         in_specs=[pl.BlockSpec(memory_space=pltpu.VMEM)] * 2,
         out_specs=[pl.BlockSpec(memory_space=pltpu.HBM)] * 2,
-        scratch_shapes=[sem((4,))],
+        scratch_shapes=[sem((7,))],
         name="store",
     )(*done)
     return new_velocity, jnp.swapaxes(new_vel, 2, 3)

time: 27 us -> 27 us (level)
  no operation moved by 1% of the time
where the time goes in v5:
time: 27 us; the launch traced here: 26.8 us
  Pallas kernels  26.2 us (97%)
  between operations  0.64 us (2%)
    pallas_call x1, Pallas kernels, body(): pl.pallas_call(functools.partial(kernel, (ns, na)), out_shape=(pltpu.VMEM...  25.3 us
    pallas_call x1, Pallas kernels, body(): pl.pallas_call(store, out_shape=tuple((pltpu.HBM(x.shape, x.dtype) for x...  0.94 us

profile of v5, /device:TPU:256, one launch (start us, length us, event | category | flops | bytes accessed | tf_op | source)
XLA Modules:
  0.0 26.8 jit_solution(1145223176926721690)
XLA Ops:
  0.6 25.3 %substep.1 = (f32[3,2,256,128]{3,2,1,0:T(8,128)S(1)}, f32[1,1,3,16,128]{4,3,2,1,0:T(8,128)S(1)}) custom-call(f32[3,2,256,128]{3,2,1,0:T(8,128)} %vel.1, f32[256]{0:T(256)} %mean.1, s32[1,1,16,128]{3,2,1,0:T(8,128)} %part_x.1, s32[1,1,16,128]{3,2,1,0:T(8,128)} %part_r.1, s32[1,1,16,128]{3,2,1,0:T(8,128)} %part_t.1, f32[1,1,3,16,128]{4,3,2,1,0:T(8,128)} %bitcast.2, ...), custom_call_target="tpu_custom_call" | custom-call | tf_op jit(solution)/shard_map/substep/pallas_call | solution.py:303
  25.9 0.9 %store.1 = (f32[3,2,256,128]{3,2,1,0:T(8,128)}, f32[1,1,3,16,128]{4,3,2,1,0:T(8,128)}) custom-call(f32[3,2,256,128]{3,2,1,0:T(8,128)S(1)} %get-tuple-element.6.velocity, f32[1,1,3,16,128]{4,3,2,1,0:T(8,128)S(1)} %get-tuple-element.7.part_vel), custom_call_target="tpu_custom_call" | custom-call | tf_op jit(solution)/shard_map/store/pallas_call | solution.py:327

commit v6 on v5

--- a/solution.py
+++ b/solution.py
@@ -9,7 +9,7 @@
 
 MESH = pl.DeviceIdType.MESH
 F32, BF16, I32 = jnp.float32, jnp.bfloat16, jnp.int32
-GROUP, PARTS, RELAYS = 4, 4, 2
+GROUP, PARTS, RELAYS = 4, 8, 2
 
 
 def iota(shape, dim):
@@ -95,33 +95,36 @@
         to = (left if d else right, a)
         return remote(vel.at[:, 1 - d, at], planes.at[d, :, at], plane_send.at[d, n], plane_recv.at[d, n], to)
 
-    def first_leg(d, n):
-        at = pl.ds((PARTS - n) * part, part)
+    def first_leg(d, n, m):
+        k = PARTS - 2 * n + m
+        at = pl.ds(k * part, part)
         to = (left - 2 * n if d else right + 2 * n, a)
-        return remote(vel.at[:, 1 - d, at], passing, plane_send.at[d, PARTS - n], pass_recv.at[0], to)
-
-    def second_leg():
-        n = PARTS - away
-        at = pl.ds(pl.multiple_of(n * part, part), part)
+        return remote(vel.at[:, 1 - d, at], passing.at[m], plane_send.at[d, k], pass_recv.at[m], to)
+
+    def second_leg(m):
+        k = PARTS - 2 * away + m
+        at = pl.ds(pl.multiple_of(k * part, part), part)
         d = jnp.where(upper, 1, 0)
         to = (jnp.where(upper, end, s - p), a)
-        return remote(passing, planes.at[d, :, at], pass_send.at[0], plane_recv.at[d, n], to)
+        return remote(passing.at[m], planes.at[d, :, at], pass_send.at[m], plane_recv.at[d, k], to)
 
     def send_planes(d):
         for n in range(PARTS):
             plane(d, n).start()
 
     def send_far(d):
-        for n in reversed(range(1, RELAYS + 1)):
-            first_leg(d, n).start()
+        for m in range(2):
+            for n in reversed(range(1, RELAYS + 1)):
+                first_leg(d, n, m).start()
 
     def send_rest(d):
-        for n in range(PARTS - RELAYS):
+        for n in range(PARTS - 2 * RELAYS):
             plane(d, n).start()
 
     def pass_on():
-        first_leg(0, 1).wait_recv()
-        second_leg().start()
+        for m in range(2):
+            first_leg(0, 1, m).wait_recv()
+            second_leg(m).start()
 
     def record(i, src, dst, send, recv, slot):
         count = 6 if src is msg else 3
@@ -279,7 +282,8 @@
         edges[d].wait_send()
         for n in range(PARTS):
             plane(d, n).wait_send()
-    pl.when(relay)(lambda: second_leg().wait_send())
+    for m in range(2):
+        pl.when(relay)(lambda: second_leg(m).wait_send())
 
 
 def store(velocity, part_vel, out_v, out_p, sems):
@@ -318,7 +322,7 @@
             pltpu.VMEM((rows, na * nt), BF16),
             pltpu.VMEM((2, 3 * nt, na * nt), BF16),
             sem((8,)), pltpu.SemaphoreType.REGULAR((na,)), pltpu.SemaphoreType.REGULAR((2,)),
-            pltpu.VMEM((3, nr // PARTS, nt), F32), sem((1,)), sem((1,)), sem((2, PARTS)), sem((2, PARTS)), sem((na,)), sem((na,)), sem((na,)), sem((na,)), sem((2,)), sem((2,)),
+            pltpu.VMEM((2, 3, nr // PARTS, nt), F32), sem((2,)), sem((2,)), sem((2, PARTS)), sem((2, PARTS)), sem((na,)), sem((na,)), sem((na,)), sem((na,)), sem((2,)), sem((2,)),
         ],
         compiler_params=pltpu.CompilerParams(collective_id=0, has_side_effects=True, vmem_limit_bytes=48 * 1024 * 1024),
         name="substep",

time: 27 us -> 27.2 us (level)
  no operation moved by 1% of the time
where the time goes in v6:
time: 27.2 us; the launch traced here: 27.1 us
  Pallas kernels  26.4 us (97%)
  between operations  0.64 us (2%)
    pallas_call x1, Pallas kernels, body(): pl.pallas_call(functools.partial(kernel, (ns, na)), out_shape=(pltpu.VMEM...  25.5 us
    pallas_call x1, Pallas kernels, body(): pl.pallas_call(store, out_shape=tuple((pltpu.HBM(x.shape, x.dtype) for x...  0.94 us

profile of v6, /device:TPU:256, one launch (start us, length us, event | category | flops | bytes accessed | tf_op | source)
XLA Modules:
  0.0 27.1 jit_solution(10046115493627814881)
XLA Ops:
  0.6 25.5 %substep.1 = (f32[3,2,256,128]{3,2,1,0:T(8,128)S(1)}, f32[1,1,3,16,128]{4,3,2,1,0:T(8,128)S(1)}) custom-call(f32[3,2,256,128]{3,2,1,0:T(8,128)} %vel.1, f32[256]{0:T(256)} %mean.1, s32[1,1,16,128]{3,2,1,0:T(8,128)} %part_x.1, s32[1,1,16,128]{3,2,1,0:T(8,128)} %part_r.1, s32[1,1,16,128]{3,2,1,0:T(8,128)} %part_t.1, f32[1,1,3,16,128]{4,3,2,1,0:T(8,128)} %bitcast.2, ...), custom_call_target="tpu_custom_call" | custom-call | tf_op jit(solution)/shard_map/substep/pallas_call | solution.py:307
  26.1 0.9 %store.1 = (f32[3,2,256,128]{3,2,1,0:T(8,128)}, f32[1,1,3,16,128]{4,3,2,1,0:T(8,128)}) custom-call(f32[3,2,256,128]{3,2,1,0:T(8,128)S(1)} %get-tuple-element.6.velocity, f32[1,1,3,16,128]{4,3,2,1,0:T(8,128)S(1)} %get-tuple-element.7.part_vel), custom_call_target="tpu_custom_call" | custom-call | tf_op jit(solution)/shard_map/store/pallas_call | solution.py:331
